TPU v7x, 256 devices: a whole 4x4x8 slice. The times are simulated.
256 devices in a mesh: leaf: 64 (over x, z, core), level: 4 (over y).
Axes of the slice: x: 4, y: 4, z: 8, core: 2. Of those that a mesh axis runs over, the one named last changes fastest.
Arguments:
- unknowns: bfloat16 [1024, 256, 1024], P(('leaf', 'level')), may hold values from -6 to 6
- leaf_basis: bfloat16 [1024, 256, 64], P(('leaf', 'level')), may hold values from -0.375 to 0.375
- leaf_transfer: bfloat16 [1024, 64, 64], P(('leaf', 'level')), may hold values from -0.75 to 0.75
- parent_transfer: bfloat16 [256, 64, 64], P(('leaf', 'level')), may hold values from -0.75 to 0.75
- near_blocks: bfloat16 [1024, 8, 256, 256], P(('leaf', 'level')), may hold values from -0.125 to 0.125
- near_offset: int32 [1024, 8], P(('leaf', 'level')), may hold values from -4 to 4, as said below
- leaf_blocks: bfloat16 [1024, 6, 64, 64], P(('leaf', 'level')), may hold values from -0.3125 to 0.3125
- leaf_partner: int32 [1024, 6], P(('leaf', 'level')), may hold values from -4 to 4, as said below
- leaf_count: int32 [1024], P(('leaf', 'level')), may hold values from 3 to 6
- top_blocks: bfloat16 [64, 32, 64, 64], P('leaf', 'level'), may hold values from -0.125 to 0.125
- top_source: int32 [64, 32], P('leaf'), may hold values from 0 to 63
- top_count: int32 [64], P('leaf'), may hold values from 8 to 32
Outputs:
- product: float32 [1024, 256, 1024], P(('leaf', 'level'))
Inputs may be any that keep to these rules, and one draw needn't show every extreme that they name: `near_offset`: each row holds 8 different offsets, the first of them 0. `leaf_partner`: each row holds 6 different nonzero offsets. `top_source`: sources may repeat within a row.
All inputs are finite; a program needn't handle non-finite values.
Results may differ from a plain program's by a relative error of at most 0.005.
Values may be sent and summed in bfloat16 or wider, within the bound.
No kernel may reach another device: no remote copies, remote signals or barrier semaphores. Data moves between devices by JAX's collectives and lax.ppermute only.
A program may use at most 128 MiB of HBM per device.

v0:
```python
import jax
import jax.numpy as jnp
from jax import lax
from jax.sharding import PartitionSpec as P


def padded(cells, sides, width):
    for axis, dim in sides:
        count = lax.axis_size(axis)
        ends = count - 1
        head = lax.slice_in_dim(cells, 0, width, axis=dim)
        tail = lax.slice_in_dim(cells, cells.shape[dim] - width, cells.shape[dim], axis=dim)
        cells = jnp.concatenate(
            [
                lax.ppermute(tail, axis, [(i, (i + 1) % count) for i in range(ends)]),
                cells,
                lax.ppermute(head, axis, [((i + 1) % count, i) for i in range(ends)]),
            ],
            axis=dim,
        )
    return cells


def body(
    unknowns,
    leaf_basis,
    leaf_transfer,
    parent_transfer,
    near_blocks,
    near_offset,
    leaf_blocks,
    leaf_partner,
    leaf_count,
    top_blocks,
    top_source,
    top_count,
):
    high = lax.Precision.HIGHEST
    local_leaves = unknowns.shape[0]
    leaf_size = unknowns.shape[1]
    leaf_moment = jnp.einsum(
        "glr,gln->grn", leaf_basis, unknowns, preferred_element_type=jnp.float32
    ).astype(jnp.bfloat16)
    stacked = jnp.concatenate([unknowns, leaf_moment], axis=1)
    window = padded(stacked, ((("leaf", "level"), 0),), local_leaves)
    centre = jnp.arange(local_leaves, dtype=jnp.int32)[:, None] + local_leaves
    near_rows = jnp.take(window[:, :leaf_size], centre + near_offset, axis=0)
    near_sum = jnp.einsum(
        "gsab,gsbn->gan", near_blocks, near_rows, preferred_element_type=jnp.float32
    )
    slot_count = leaf_partner.shape[1]
    live_mask = (jnp.arange(slot_count, dtype=jnp.int32)[None, :] < leaf_count[:, None]).astype(
        jnp.bfloat16
    )
    partner_rows = (
        jnp.take(window[:, leaf_size:], centre + leaf_partner, axis=0) * live_mask[:, :, None, None]
    )
    leaf_far = jnp.einsum(
        "gsab,gsbn->gan", leaf_blocks, partner_rows, preferred_element_type=jnp.float32
    )
    parent_moment = jnp.einsum(
        "krs,krn->sn", leaf_transfer, leaf_moment, preferred_element_type=jnp.float32
    ).astype(jnp.bfloat16)
    root_terms = jnp.einsum(
        "rs,rn->sn", parent_transfer[0], parent_moment, preferred_element_type=jnp.float32
    )
    root_moment = lax.psum(root_terms, "level").astype(jnp.bfloat16)
    all_roots = lax.all_gather(root_moment[None], "leaf", axis=0, tiled=True)
    per_level = top_blocks.shape[1]
    first_slot = lax.axis_index("level") * per_level
    slot_index = first_slot + jnp.arange(per_level, dtype=jnp.int32)
    sources = lax.dynamic_slice_in_dim(top_source[0], first_slot, per_level)
    slot_live = (slot_index < top_count[0]).astype(jnp.bfloat16)
    picked = jnp.take(all_roots, sources, axis=0) * slot_live[:, None, None]
    partial_value = jnp.einsum(
        "kab,kbn->an", top_blocks[0], picked, preferred_element_type=jnp.float32
    )
    root_field = lax.psum(partial_value, "level")
    parent_field = jnp.dot(parent_transfer[0].astype(jnp.float32), root_field, precision=high)
    leaf_field = (
        jnp.einsum("krs,sn->krn", leaf_transfer.astype(jnp.float32), parent_field, precision=high)
        + leaf_far
    )
    leaf_field = leaf_field.astype(jnp.bfloat16)
    return (
        jnp.einsum("glr,grn->gln", leaf_basis, leaf_field, preferred_element_type=jnp.float32)
        + near_sum
    )


def solution(mesh):
    return jax.shard_map(
        body,
        mesh=mesh,
        in_specs=(
            P(("leaf", "level"), None, None),
            P(("leaf", "level"), None, None),
            P(("leaf", "level"), None, None),
            P(("leaf", "level"), None, None),
            P(("leaf", "level"), None, None, None),
            P(("leaf", "level"), None),
            P(("leaf", "level"), None, None, None),
            P(("leaf", "level"), None),
            P(("leaf", "level")),
            P("leaf", "level", None, None),
            P("leaf", None),
            P("leaf"),
        ),
        out_specs=P(("leaf", "level"), None, None),
        check_vma=False,
    )
```

profile of v0, /device:TPU:2, one launch (start us, length us, event | category | flops | bytes accessed | tf_op | source)
XLA Modules:
  0.0 200.7 jit_solution(14624868585861354076)
XLA Ops:
  6.6 0.0 all-gather.3.cloned.1.call-start
  6.6 2.3 %convolution_convert_fusion = bf16[4,64,1024]{2,1,0:T(8,128)(2,1)S(1)} fusion(bf16[4,256,64]{1,2,0:T(8,128)(2,1)} %param.13, bf16[4,256,1024]{2,1,0:T(8,128)(2,1)} %param.12), kind=kOutput, calls=%fused_computation.25 | convolution fusion | flops 134479872 | bytes 2752512 | tf_op jit(solution)/shard_map/glr,gln->grn/dot_general | solution.py:41
  8.9 0.0 copy-start.8
  8.9 1.4 fusion.27
  10.3 20.6 %all-reduce.4 = bf16[64,1024]{1,0:T(8,128)(2,1)} all-reduce(f32[64,1024]{1,0:T(8,128)S(1)} %fusion.27), channel_id=1, replica_groups=mesh['leaf'=64,'level'=4] {'level'}, use_global_device_ids=true, to_apply=%region_0.1 | all-reduce | flops 65536 | bytes 393216 | tf_op jit(solution)/shard_map/psum | solution.py:67
  30.9 0.0 all-gather.3.cloned.1.call-update
  31.0 0.0 all-reduce.3.cloned.1.call-start
  31.0 1.8 pad_maximum_fusion.3
  32.8 3.1 %collective-permute-start.1 = (bf16[4,320,1024]{2,1,0:T(8,128)(2,1)}, bf16[4,320,1024]{2,1,0:T(8,128)(2,1)}, u32[]{:S(2)}, u32[]{:S(2)}) collective-permute-start(bf16[4,320,1024]{2,1,0:T(8,128)(2,1)} %pad_maximum_fusion.3), channel_id=1, source_target_pairs={{1,0},{2,1},{3,2},{4,3},{5,4},{6,5},{7,6},{8,7},{9,8},{10,9},{11,1... | collective-permute-start | bytes 7864328 | tf_op jit(solution)/shard_map/ppermute | solution.py:17
  35.9 2.7 %collective-permute-start = (bf16[4,320,1024]{2,1,0:T(8,128)(2,1)}, bf16[4,320,1024]{2,1,0:T(8,128)(2,1)}, u32[]{:S(2)}, u32[]{:S(2)}) collective-permute-start(bf16[4,320,1024]{2,1,0:T(8,128)(2,1)} %pad_maximum_fusion.3), channel_id=1, source_target_pairs={{0,1},{1,2},{2,3},{3,4},{4,5},{5,6},{6,7},{7,8},{8,9},{9,10},{10,1... | collective-permute-start | bytes 7864328 | tf_op jit(solution)/shard_map/ppermute | solution.py:15
  39.3 0.1 compare_and_fusion
  39.4 0.1 reshape.96
  39.5 0.1 compare_and_fusion.1
  39.5 0.1 reshape.88
  39.6 0.1 fusion.37
  39.7 0.1 compare_convert_fusion
  39.8 0.1 fusion.36
  39.9 74.3 %all-gather.3.cloned.1.call-done = bf16[4096,1024]{1,0:T(8,128)(2,1)} async-done(((bf16[64,1024]{1,0:T(8,128)(2,1)}), bf16[4096,1024]{1,0:T(8,128)(2,1)}) %all-gather.3.cloned.1.call-update) | async-done | bytes 8388624 | tf_op jit(solution)/shard_map/all_gather | solution.py:68
  114.2 5.1 %gather_fusion = bf16[8,64,1024]{2,1,0:T(8,128)(2,1)} fusion(bf16[64,64,1024]{2,1,0:T(8,128)(2,1)} %bitcast.67, s32[1024]{0:T(1024)S(1)} %pad_clamp_fusion.2), kind=kCustom, calls=%fused_computation | custom fusion | bytes 2097184 | tf_op jit(solution)/shard_map/jit(_take)/gather | solution.py:74
  119.2 2.9 %convolution_bitcast_fusion.2 = f32[64,1024]{0,1:T(8,128)} fusion(bf16[8,64,1024]{2,1,0:T(8,128)(2,1)} %gather_fusion, pred[8]{0:T(512)(128)(4,1)S(1)} %get-tuple-element.10, bf16[8]{0:T(256)(128)(2,1)S(1)} %get-tuple-element.9, bf16[1,8,64,64]{3,2,1,0:T(8,128)(2,1)S(1)} %copy-done.8), kind=kOutput, calls=%fused_computation.27 | convolution fusion | flops 68157440 | bytes 1376280 | tf_op jit(solution)/shard_map/kab,kbn->an/dot_general | solution.py:75
  122.1 0.0 all-reduce.3.cloned.1.call-update
  122.2 5.5 %pad_maximum_fusion = bf16[12,256,1024]{2,1,0:T(8,128)(2,1)} fusion(bf16[4,320,1024]{2,1,0:T(8,128)(2,1)} %collective-permute-done.1, bf16[4,320,1024]{2,1,0:T(8,128)(2,1)} %collective-permute-done, bf16[4,64,1024]{2,1,0:T(8,128)(2,1)S(1)} %convolution_convert_fusion, bf16[4,256,1024]{2,1,0:T(8,128)(2,1)S(1)} %copy-done.1), kind=kLoop, calls=%fused_computation.7 | loop fusion | flops 25165824 | bytes 14155776 | tf_op jit(solution)/shard_map/concatenate | solution.py:13
  127.7 10.1 %gather_fusion.2 = bf16[32,256,1024]{2,1,0:T(8,128)(2,1)} fusion(bf16[12,256,1024]{2,1,0:T(8,128)(2,1)} %pad_maximum_fusion, s32[1024]{0:T(1024)S(1)} %pad_clamp_fusion), kind=kCustom, calls=%fused_computation.2 | custom fusion | bytes 33554560 | tf_op jit(solution)/shard_map/jit(_take)/gather | solution.py:47
  137.8 21.8 %copy.13 = bf16[4,8,256,1024]{2,3,1,0:T(8,128)(2,1)} copy(bf16[4,8,256,1024]{3,2,1,0:T(8,128)(2,1)} %bitcast.65) | data formatting | bytes 33554432 | tf_op jit(solution)/shard_map/jit(_take)/gather | solution.py:47
  159.6 2.5 %pad_maximum_fusion.4 = bf16[12,64,1024]{2,1,0:T(8,128)(2,1)} fusion(bf16[4,320,1024]{2,1,0:T(8,128)(2,1)} %collective-permute-done.1, bf16[4,320,1024]{2,1,0:T(8,128)(2,1)} %collective-permute-done, bf16[4,64,1024]{2,1,0:T(8,128)(2,1)S(1)} %convolution_convert_fusion, bf16[4,256,1024]{2,1,0:T(8,128)(2,1)S(1)} %copy-done.1), kind=kLoop, calls=%fused_computation.17 | loop fusion | flops 6291456 | bytes 9437184 | tf_op jit(solution)/shard_map/slice | solution.py:56
  162.1 3.9 %gather_fusion.1 = bf16[24,64,1024]{2,1,0:T(8,128)(2,1)} fusion(bf16[12,64,1024]{2,1,0:T(8,128)(2,1)} %pad_maximum_fusion.4, s32[1024]{0:T(1024)S(1)} %pad_clamp_fusion.1), kind=kCustom, calls=%fused_computation.1 | custom fusion | bytes 6291552 | tf_op jit(solution)/shard_map/jit(_take)/gather | solution.py:56
  166.1 2.9 %all-reduce.3.cloned.1.call-done = f32[64,1024]{0,1:T(8,128)} async-done(((f32[64,1024]{0,1:T(8,128)}), f32[64,1024]{0,1:T(8,128)}) %all-reduce.3.cloned.1.call-update) | async-done | bytes 262160 | tf_op jit(solution)/shard_map/psum | solution.py:78
  169.0 1.4 convolution_bitcast_fusion.1
  170.4 0.6 convolution_bitcast_fusion
  171.0 5.6 %fusion.23 = f32[4,1024,256]{2,1,0:T(8,128)} fusion(bf16[4,256,64]{1,2,0:T(8,128)(2,1)S(1)} %copy-done.2, f32[4,64,1024]{2,1,0:T(8,128)S(1)} %convolution_bitcast_fusion, bf16[4,6,64,64]{3,2,1,0:T(8,128)(2,1)S(1)} %copy-done, bf16[4,6,64,1024]{3,2,1,0:T(8,128)(2,1)} %bitcast.66, pred[4,6]{1,0:T(4,128)(4,1)S(1)} %get-tuple-element.7, ...), kind=kOutput, calls=%fused_computation.24 | convolution fusion | flops 343932928 | bytes 8716360 | tf_op jit(solution)/shard_map/glr,grn->gln/dot_general | solution.py:86
  176.6 11.9 %fusion.4 = f32[4,256,1024]{1,2,0:T(8,128)} fusion(f32[4,1024,256]{2,1,0:T(8,128)} %fusion.23, bf16[4,8,256,256]{3,2,1,0:T(8,128)(2,1)} %param.16, bf16[4,8,256,1024]{2,3,1,0:T(8,128)(2,1)} %copy.13, pred[4,8]{1,0:T(4,128)(4,1)S(1)} %get-tuple-element.5), kind=kOutput, calls=%fused_computation.11 | convolution fusion | flops 4304404480 | bytes 29360160 | tf_op jit(solution)/shard_map/gsab,gsbn->gan/dot_general | solution.py:48
  188.5 5.3 %copy.14 = f32[4,256,1024]{2,1,0:T(8,128)} copy(f32[4,256,1024]{1,2,0:T(8,128)} %fusion.4) | data formatting | bytes 8388608 | tf_op jit(solution)/shard_map/add | solution.py:86
  (25 shorter events, 0.1 us)
Async XLA Ops:
  6.5 164.5 %copy-start = (bf16[4,6,64,64]{3,2,1,0:T(8,128)(2,1)S(1)}, bf16[4,6,64,64]{3,2,1,0:T(8,128)(2,1)}, u32[]{:S(2)}) copy-start(bf16[4,6,64,64]{3,2,1,0:T(8,128)(2,1)} %param.18) | copy-start | bytes 589828
  6.5 24.5 %copy-start.1 = (bf16[4,256,1024]{2,1,0:T(8,128)(2,1)S(1)}, bf16[4,256,1024]{2,1,0:T(8,128)(2,1)}, u32[]{:S(2)}) copy-start(bf16[4,256,1024]{2,1,0:T(8,128)(2,1)} %param.12) | copy-start | bytes 6291460
  6.5 32.7 %copy-start.5 = (s32[4,8]{1,0:T(4,128)S(1)}, s32[4,8]{1,0:T(4,128)}, u32[]{:S(2)}) copy-start(s32[4,8]{1,0:T(4,128)} %param.17) | copy-start | bytes 388
  6.5 32.9 %copy-start.6 = (s32[4,6]{1,0:T(4,128)S(1)}, s32[4,6]{1,0:T(4,128)}, u32[]{:S(2)}) copy-start(s32[4,6]{1,0:T(4,128)} %param.19) | copy-start | bytes 292
  6.5 33.1 %copy-start.7 = (s32[1,32]{1,0:T(1,128)S(1)}, s32[1,32]{1,0:T(1,128)}, u32[]{:S(2)}) copy-start(s32[1,32]{1,0:T(1,128)} %param.22) | copy-start | bytes 388
  6.5 33.3 %copy-start.9 = (s32[4]{0:T(128)S(1)}, s32[4]{0:T(128)}, u32[]{:S(2)}) copy-start(s32[4]{0:T(128)} %param.20) | copy-start | bytes 52
  6.6 107.6 %all-gather.3.cloned.1.call-start = ((), (), s32[]{:S(2)}) async-start(), calls=%async_computation.1 | async-start | bytes 8519680 | tf_op jit(solution)/shard_map/all_gather | solution.py:68
  8.9 110.3 %copy-start.8 = (bf16[1,8,64,64]{3,2,1,0:T(8,128)(2,1)S(1)}, bf16[1,8,64,64]{3,2,1,0:T(8,128)(2,1)}, u32[]{:S(2)}) copy-start(bf16[1,8,64,64]{3,2,1,0:T(8,128)(2,1)} %param.21) | copy-start | bytes 196612
  31.0 138.0 %all-reduce.3.cloned.1.call-start = ((), (), s32[]{:S(2)}) async-start(), calls=%async_computation | async-start | bytes 1048576 | tf_op jit(solution)/shard_map/psum | solution.py:78
  32.8 89.4 %collective-permute-start.1 = (bf16[4,320,1024]{2,1,0:T(8,128)(2,1)}, bf16[4,320,1024]{2,1,0:T(8,128)(2,1)}, u32[]{:S(2)}, u32[]{:S(2)}) collective-permute-start(bf16[4,320,1024]{2,1,0:T(8,128)(2,1)} %pad_maximum_fusion.3), channel_id=1, source_target_pairs={{1,0},{2,1},{3,2},{4,3},{5,4},{6,5},{7,6},{8,7},{9,8},{10,9},{11,1... | collective-permute-start | bytes 7864328 | tf_op jit(solution)/shard_map/ppermute | solution.py:17
  35.9 86.2 %collective-permute-start = (bf16[4,320,1024]{2,1,0:T(8,128)(2,1)}, bf16[4,320,1024]{2,1,0:T(8,128)(2,1)}, u32[]{:S(2)}, u32[]{:S(2)}) collective-permute-start(bf16[4,320,1024]{2,1,0:T(8,128)(2,1)} %pad_maximum_fusion.3), channel_id=1, source_target_pairs={{0,1},{1,2},{2,3},{3,4},{4,5},{5,6},{6,7},{7,8},{8,9},{9,10},{10,1... | collective-permute-start | bytes 7864328 | tf_op jit(solution)/shard_map/ppermute | solution.py:15
  162.1 6.9 %copy-start.4 = (bf16[1,64,64]{2,1,0:T(8,128)(2,1)S(1)}, bf16[1,64,64]{2,1,0:T(8,128)(2,1)}, u32[]{:S(2)}) copy-start(bf16[1,64,64]{2,1,0:T(8,128)(2,1)} %param.15) | copy-start | bytes 24580
  162.1 8.3 %copy-start.3 = (bf16[4,64,64]{2,1,0:T(8,128)(2,1)S(1)}, bf16[4,64,64]{2,1,0:T(8,128)(2,1)}, u32[]{:S(2)}) copy-start(bf16[4,64,64]{2,1,0:T(8,128)(2,1)} %param.14) | copy-start | bytes 98308
  162.1 8.9 %copy-start.2 = (bf16[4,256,64]{1,2,0:T(8,128)(2,1)S(1)}, bf16[4,256,64]{1,2,0:T(8,128)(2,1)}, u32[]{:S(2)}) copy-start(bf16[4,256,64]{1,2,0:T(8,128)(2,1)} %param.13) | copy-start | bytes 393220
Sparse Core Ops, SparseCore 0:
  31.1 83.0 all-gather.2
  122.3 46.6 all-reduce.2
where the time goes:
time: 202 us; the launch traced here: 201 us
  waiting for transfers between devices  77.2 us (38%)
  local copies, waits for them, and re-layouts  46.5 us (23%)
  matrix products  26.1 us (13%)
  blocking collectives  20.6 us (10%)
  between operations  14.2 us (7%)
  other arithmetic  10.2 us (5%)
  starting transfers between devices  5.91 us (3%)
    all_gather x1, waiting for transfers between devices, body(): all_roots = lax.all_gather(root_moment[None], 'leaf', axis=0, tiled=True)  74.3 us
    gather x2, local copies, waits for them, and re-layouts, body(): near_rows = jnp.take(window[:, :leaf_size], centre + near_offset, axis=0)  31.9 us
    psum x1, blocking collectives, body(): root_moment = lax.psum(root_terms, 'level').astype(jnp.bfloat16)  20.6 us
    dot_general x1, matrix products, body(): jnp.einsum('gsab,gsbn->gan', near_blocks, near_rows, preferred_element_ty...  11.9 us
    dot_general x1, matrix products, body(): jnp.einsum('glr,grn->gln', leaf_basis, leaf_field, preferred_element_type...  5.6 us
    concatenate x1, other arithmetic, padded(): jnp.concatenate([lax.ppermute(tail, axis, [(i, (i + 1) % count) for i in...  5.49 us
    add x1, local copies, waits for them, and re-layouts, body(): jnp.einsum('glr,grn->gln', leaf_basis, leaf_field, preferred_element_type...  5.34 us
    gather x1, local copies, waits for them, and re-layouts, body(): picked = jnp.take(all_roots, sources, axis=0) * slot_live[:, None, None]  5.05 us
  transfers between devices with their start and end apart: 4, of which 2 were waited for; matrix products, arithmetic and copies ran while one was open for 27% of the time, Pallas kernels for 0%

commit v1 on v0

v1 whole, which is shorter than its diff:
```python
import functools

import jax
import jax.numpy as jnp
from jax import lax
from jax.experimental import pallas as pl
from jax.experimental.pallas import tpu as pltpu
from jax.sharding import PartitionSpec as P

X, Z, CORES = 4, 8, 2
LEVEL = 4
BF = jnp.bfloat16
F32 = jnp.float32
MIB = 1 << 20

OWN = (4, 5, 6, 7)
HALO = (0, 1, 2, 3, 8, 9, 10, 11)


def dot(a, b, dims=((1,), (0,))):
    return lax.dot_general(a, b, (dims, ((), ())), preferred_element_type=F32)


def near_block(slot_ref, nb_ref, target, place):
    slot = slot_ref[target, place - target]
    block = nb_ref[target, jnp.maximum(slot, 0)]
    return jnp.where(slot >= 0, block, jnp.zeros_like(block))


def moments_kernel(
    u_ref, bt_ref, lt_ref, pt_ref, tb_ref, msg_ref, out_ref, m_ref, u, bt, lt, pt, tb, sem, out_sem
):
    small = [
        pltpu.make_async_copy(src, dst, sem.at[4 + n])
        for n, (src, dst) in enumerate(((bt_ref, bt), (lt_ref, lt), (pt_ref, pt), (tb_ref, tb)))
    ]
    large = [pltpu.make_async_copy(u_ref.at[g], u.at[g], sem.at[g]) for g in range(4)]
    outward = [
        pltpu.make_async_copy(u.at[g], out_ref.at[256 * g : 256 * (g + 1)], out_sem.at[g]) for g in range(4)
    ]
    outward += [
        pltpu.make_async_copy(bt.at[g], out_ref.at[1024:1088, 256 * g : 256 * (g + 1)], out_sem.at[4 + g])
        for g in range(4)
    ]
    small[0].start()
    for copy in large + small[1:]:
        copy.start()
    small[0].wait()
    for g in range(4):
        outward[4 + g].start()
    for g in range(4):
        large[g].wait()
        outward[g].start()
        m_ref[64 * g : 64 * (g + 1)] = dot(bt[g], u[g]).astype(BF)
    for copy in small[1:]:
        copy.wait()
    parent = dot(lt[...], m_ref[...], ((0,), (0,))).astype(BF)
    packed = jnp.concatenate([pt[16 * j : 16 * (j + 1)] for j in range(4)], axis=1)
    blocks = [jnp.concatenate([tb[4 * half + s] for s in range(4)], axis=1) for half in range(2)]
    for q in range(LEVEL):
        msg_ref[q, 0:64] = parent[:, 256 * q : 256 * (q + 1)]
        msg_ref[q, 64:128] = blocks[0]
        msg_ref[q, 128:192] = blocks[1]
        msg_ref[q, 192:208] = packed
    for copy in outward:
        copy.wait()


def roots_kernel(msg_ref, after_ref, out_ref, held, sem):
    copies = [
        pltpu.make_async_copy(msg_ref.at[k, at : at + size], held.at[k, to : to + size], sem.at[k, n])
        for k in range(LEVEL)
        for n, (at, size, to) in enumerate(((0, 64, 0), (192, 16, 64)))
    ]
    for copy in copies:
        copy.start()
    for copy in copies:
        copy.wait()
    total = jnp.zeros((64, 256), F32)
    for k in range(LEVEL):
        packed = held[k, 64:80]
        pt = jnp.concatenate([packed[:, 64 * j : 64 * (j + 1)] for j in range(4)], axis=0)
        total += dot(pt, held[k, 0:64], ((0,), (0,)))
    root = total.astype(BF)
    for z in range(Z):
        out_ref[z] = root


def after_kernel(*refs):
    pass


def ordered(arrays, after, name):
    return pl.pallas_call(
        after_kernel,
        in_specs=[HBM] * (len(arrays) + len(after)),
        out_specs=[HBM] * len(arrays),
        out_shape=[jax.ShapeDtypeStruct(array.shape, array.dtype) for array in arrays],
        input_output_aliases={n: n for n in range(len(arrays))},
        compiler_params=params(60),
        name=name,
    )(*arrays, *after)


def crossing_kernel(u_ref, bt_ref, after_ref, out_ref, held, sem):
    rows = [(256 * g, 256) for g in range(4)] + [(1024, 64)]
    inward = [pltpu.make_async_copy(u_ref.at[g], held.at[256 * g : 256 * (g + 1)], sem.at[0, g]) for g in range(4)]
    inward += [
        pltpu.make_async_copy(bt_ref.at[g], held.at[1024:1088, 256 * g : 256 * (g + 1)], sem.at[0, 4 + g])
        for g in range(4)
    ]
    outward = [
        pltpu.make_async_copy(held.at[at : at + size], out_ref.at[at : at + size], sem.at[1, n])
        for n, (at, size) in enumerate(rows)
    ]
    for copy in inward:
        copy.start()
    for g in range(4):
        inward[g].wait()
        outward[g].start()
    for copy in inward[4:]:
        copy.wait()
    outward[4].start()
    for copy in outward:
        copy.wait()


def near_kernel(
    offset_ref, partner_ref, count_ref, u_hbm, nb_hbm, lb_hbm, bt_hbm, p_hbm, n_hbm,
    acc_out, blocks_out, left_out, slot_ref, far_slot, u, nb, lb, bt, p, n, blocks, left, acc, sem, out_sem,
):
    def load(src, dst, at):
        copy = pltpu.make_async_copy(src, dst, sem.at[at])
        copy.start()
        return copy

    small = [load(lb_hbm, lb, 0), load(bt_hbm, bt, 1)]
    small += [load(p_hbm.at[1024:1088], p.at[1024:1088], 2), load(n_hbm.at[1024:1088], n.at[1024:1088], 3)]
    tables = [load(nb_hbm.at[0], nb.at[0], 4)]
    large = [load(u_hbm, u, 8), load(p_hbm.at[0:1024], p.at[0:1024], 9), load(n_hbm.at[0:1024], n.at[0:1024], 10)]
    tables += [load(nb_hbm.at[i], nb.at[i], 4 + i) for i in range(1, 4)]
    for i in range(4):
        for o in range(9):
            slot_ref[i, o] = -1
            far_slot[i, o] = -1
        for s in range(8):
            slot_ref[i, offset_ref[i, s] + 4] = s
        for s in range(6):

            @pl.when(s < count_ref[i])
            def _():
                far_slot[i, partner_ref[i, s] + 4] = s

    for copy in small:
        copy.wait()
    zero = jnp.zeros((64, 64), BF)
    outward = []
    for i in range(4):
        rows = slice(256 * i, 256 * (i + 1))
        places = list(range(i, 4)) + list(range(8, i + 9)) + [w for w in OWN if w != i + 4]
        coupling = []
        for w in places:
            slot = far_slot[i, w - i]
            coupling.append(jnp.where(slot >= 0, lb[i, jnp.maximum(slot, 0)], zero))
        left_i = dot(bt[i].T, jnp.concatenate(coupling, axis=1)).astype(BF)
        left[rows] = left_i[:, 0:320]
        tables[i].wait()
        for k, w in enumerate(places):
            if w in OWN:
                other, at = bt[w - 4], 1280 + 256 * (w - 4)
            else:
                ref, g = (p, w) if w < 4 else (n, w - 8)
                other, at = ref[1024:1088, 256 * g : 256 * (g + 1)], 256 * k
            block = near_block(slot_ref, nb, i, w).astype(F32) + dot(left_i[:, 64 * k : 64 * (k + 1)], other)
            blocks[rows, at : at + 256] = block.astype(BF)
        blocks[rows, 1280 + 256 * i : 1536 + 256 * i] = near_block(slot_ref, nb, i, i + 4)
        if i == 0:
            for copy in large:
                copy.wait()
        for half in range(2):
            cols = slice(512 * half, 512 * (half + 1))
            sources = [p[256 * w : 256 * (w + 1), cols] for w in range(i, 4)]
            sources += [n[256 * w : 256 * (w + 1), cols] for w in range(i + 1)]
            sources += [u[w, :, cols] for w in range(4)]
            acc[i, :, cols] = dot(blocks[rows], jnp.concatenate(sources, axis=0))
        outward.append(pltpu.make_async_copy(acc.at[i], acc_out.at[i], out_sem.at[i]))
        outward[-1].start()
    outward.append(pltpu.make_async_copy(blocks.at[:, 0:1280], blocks_out, out_sem.at[4]))
    outward[-1].start()
    outward.append(pltpu.make_async_copy(left, left_out, out_sem.at[5]))
    outward[-1].start()
    for copy in outward:
        copy.wait()


def top_kernel(source_ref, count_ref, own0, own1, own2, own3, other0, other1, other2, other3, msg_ref, out_ref, table, blocks, sem, block_sem):
    copies = []
    for k, pair in enumerate(((own0, other0), (own1, other1), (own2, other2), (own3, other3))):
        for c in range(CORES):
            copies.append(pltpu.make_async_copy(pair[c], table.at[c, k], sem.at[c, k]))
    for k in range(LEVEL):
        copies.append(pltpu.make_async_copy(msg_ref.at[k, 64:192], blocks.at[k], block_sem.at[k]))
    for copy in copies:
        copy.start()
    for copy in copies:
        copy.wait()
    lead = lax.axis_index("leaf")
    my_x, my_core = lead // (Z * CORES), lax.rem(lead, CORES)
    total = jnp.zeros((64, 256), F32)
    for k in range(LEVEL):
        for half in range(2):
            rows = []
            for s in range(4):
                at = 8 * k + 4 * half + s
                source = source_ref[0, at]
                core = lax.rem(source + my_core, CORES)
                step = lax.rem(my_x - source // (Z * CORES) + X, X)
                row = table[core, step, lax.rem(source // CORES, Z)]
                rows.append(jnp.where(at < count_ref[0], row, jnp.zeros_like(row)))
            total += dot(blocks[k, 64 * half : 64 * (half + 1)], jnp.concatenate(rows, axis=0))
    for k in range(LEVEL):
        out_ref[k] = total.astype(BF)


def last_kernel(
    cross_hbm, blocks_hbm, left_hbm, acc_hbm, field_hbm, lt_hbm, pt_hbm, bt_hbm, out_ref,
    cross, blocks, left, acc, field, lt, pt, bt, held, sem, out_sem,
):
    def load(src, dst, at):
        return pltpu.make_async_copy(src, dst, sem.at[at])

    small = [load(field_hbm, field, 0), load(lt_hbm, lt, 1), load(pt_hbm, pt, 2), load(bt_hbm, bt, 3)]
    large = [load(acc_hbm.at[i], acc.at[i], 4 + i) for i in range(4)]
    extra = [load(left_hbm, left, 8), load(blocks_hbm, blocks, 9), load(cross_hbm, cross, 10)]
    level = lax.axis_index("level")
    core = lax.rem(lax.axis_index("leaf"), CORES)
    cross_prev = jnp.logical_and(level == 0, core == 0)
    cross_next = jnp.logical_and(level == LEVEL - 1, core == CORES - 1)
    leaf_rows = [slice(256 * w, 256 * (w + 1)) for w in range(4)]
    sides = ((cross_prev, lambda i: range(0, 4 - i)), (cross_next, lambda i: range(4 - i, 5)))
    crossing = jnp.logical_or(cross_prev, cross_next)

    for copy in small + large:
        copy.start()

    @pl.when(crossing)
    def _():
        for copy in extra:
            copy.start()
        for copy in extra:
            copy.wait()

    for side, places in sides:

        @pl.when(side)
        def _():
            for i in range(4):
                target = leaf_rows[i]
                for n in places(i):
                    far = dot(left[target, 64 * n : 64 * (n + 1)], cross[1024:1088, leaf_rows[(i + n) % 4]])
                    block = blocks[target, 256 * n : 256 * (n + 1)].astype(F32) + far
                    blocks[target, 256 * n : 256 * (n + 1)] = block.astype(BF)

    for copy in small:
        copy.wait()
    whole = jnp.concatenate([field[q] for q in range(LEVEL)], axis=1)
    parent = dot(pt[...], whole)
    high = parent.astype(BF)
    low = (parent - high.astype(F32)).astype(BF)
    outward = []
    for i in range(4):
        basis = bt[i].T
        transfer = lt[64 * i : 64 * (i + 1)]
        leaf = dot(transfer, high) + dot(transfer, low)
        leaf_high = leaf.astype(BF)
        leaf_low = (leaf - leaf_high.astype(F32)).astype(BF)
        large[i].wait()
        held[i] = acc[i] + dot(
            jnp.concatenate([basis, basis], axis=1), jnp.concatenate([leaf_high, leaf_low], axis=0)
        )

        for side, places in sides:

            @pl.when(side)
            def _():
                reach = places(i)
                sources = [cross[leaf_rows[(i + n) % 4]] for n in reach]
                held[i] += dot(
                    blocks[leaf_rows[i], 256 * reach[0] : 256 * (reach[-1] + 1)], jnp.concatenate(sources, axis=0)
                )

        outward.append(pltpu.make_async_copy(held.at[i], out_ref.at[i], out_sem.at[i]))
        outward[-1].start()
    for copy in outward:
        copy.wait()


def params(mib):
    return pltpu.CompilerParams(vmem_limit_bytes=mib * MIB)


VMEM = pl.BlockSpec(memory_space=pltpu.VMEM)
SMEM = pl.BlockSpec(memory_space=pltpu.SMEM)
ANY = pl.BlockSpec(memory_space=pl.ANY)
HBM = pl.BlockSpec(memory_space=pltpu.HBM)


def body(
    unknowns, leaf_basis, leaf_transfer, parent_transfer, near_blocks, near_offset,
    leaf_blocks, leaf_partner, leaf_count, top_blocks, top_source, top_count,
):
    both = ("leaf", "level")
    total = lax.axis_size("leaf") * LEVEL
    ahead = [(i, i + 1) for i in range(total - 1)]
    back = [(i + 1, i) for i in range(total - 1)]

    def crossing(a):
        return a % LEVEL == LEVEL - 1 and a // LEVEL % CORES == CORES - 1

    bt = leaf_basis.transpose(0, 2, 1)
    lt = leaf_transfer.reshape(256, 64)
    pt = parent_transfer[0]

    pieces, message = pl.pallas_call(
        moments_kernel,
        in_specs=[HBM] * 5,
        out_specs=[VMEM, HBM],
        out_shape=[jax.ShapeDtypeStruct((LEVEL, 208, 256), BF), jax.ShapeDtypeStruct((1088, 1024), BF)],
        scratch_shapes=[
            pltpu.VMEM((256, 1024), BF), pltpu.VMEM((4, 256, 1024), BF), pltpu.VMEM((4, 64, 256), BF),
            pltpu.VMEM((256, 64), BF), pltpu.VMEM((64, 64), BF), pltpu.VMEM((8, 64, 64), BF),
            pltpu.SemaphoreType.DMA((8,)), pltpu.SemaphoreType.DMA((8,)),
        ],
        compiler_params=params(60),
        name="moments",
    )(unknowns, bt, lt, pt, top_blocks[0])

    heap = lax.all_to_all(pieces, "level", 0, 0, tiled=True)

    (message,) = ordered([message], [heap], "send_inner")
    inner = lambda pairs: [(a, b) for a, b in pairs if not crossing(min(a, b))]
    inner_prev = lax.ppermute(message, both, inner(ahead))
    inner_next = lax.ppermute(message, both, inner(back))

    root = pl.pallas_call(
        roots_kernel,
        in_specs=[HBM] * 2,
        out_specs=VMEM,
        out_shape=jax.ShapeDtypeStruct((Z, 64, 256), BF),
        scratch_shapes=[pltpu.VMEM((LEVEL, 80, 256), BF), pltpu.SemaphoreType.DMA((LEVEL, 2))],
        compiler_params=params(60),
        name="roots",
    )(heap, message)

    def place(x, z, c):
        return (x * Z + z) * CORES + c

    leaves = [(x, z, c) for x in range(X) for z in range(Z) for c in range(CORES)]
    along_x = lambda step: [(place(x, z, c), place((x + step) % X, z, c)) for x, z, c in leaves]
    swap = [(place(x, z, c), place(x, z, 1 - c)) for x, z, c in leaves]
    groups = [[place(x, z, c) for z in range(Z)] for x in range(X) for c in range(CORES)]
    column = lax.all_to_all(root, "leaf", 0, 0, axis_index_groups=groups, tiled=True)
    mine = [column] + [lax.ppermute(column, "leaf", along_x(step)) for step in range(1, X)]
    theirs = [lax.ppermute(m, "leaf", swap) for m in mine]
    acc_shape = jax.ShapeDtypeStruct((4, 256, 1024), F32)
    message = pl.pallas_call(
        crossing_kernel,
        in_specs=[HBM] * 3,
        out_specs=HBM,
        out_shape=jax.ShapeDtypeStruct((1088, 1024), BF),
        scratch_shapes=[pltpu.VMEM((1088, 1024), BF), pltpu.SemaphoreType.DMA((2, 8))],
        compiler_params=params(60),
        name="send_crossing",
    )(unknowns, bt, mine[1])
    cross = lax.ppermute(message, both, [(a, b) for a, b in ahead + back if crossing(min(a, b))])

    field = pl.pallas_call(
        top_kernel,
        in_specs=[SMEM, SMEM] + [HBM] * 9,
        out_specs=VMEM,
        scratch_shapes=[
            pltpu.VMEM((CORES, X, Z, 64, 256), BF), pltpu.VMEM((LEVEL, 128, 256), BF),
            pltpu.SemaphoreType.DMA((CORES, X)), pltpu.SemaphoreType.DMA((LEVEL,)),
        ],
        out_shape=jax.ShapeDtypeStruct((LEVEL, 64, 256), BF),
        compiler_params=params(60),
        name="top",
    )(top_source, top_count, *mine, *theirs, heap)
    fields = lax.all_to_all(field, "level", 0, 0, tiled=True)

    acc, blocks, left = pl.pallas_call(
        near_kernel,
        in_specs=[SMEM] * 3 + [HBM] * 6,
        out_specs=[HBM] * 3,
        out_shape=[
            acc_shape, jax.ShapeDtypeStruct((1024, 1280), BF), jax.ShapeDtypeStruct((1024, 320), BF),
        ],
        scratch_shapes=[
            pltpu.SMEM((4, 9), jnp.int32), pltpu.SMEM((4, 9), jnp.int32), pltpu.VMEM((4, 256, 1024), BF),
            pltpu.VMEM((4, 8, 256, 256), BF), pltpu.VMEM((4, 6, 64, 64), BF), pltpu.VMEM((4, 64, 256), BF),
            pltpu.VMEM((1088, 1024), BF), pltpu.VMEM((1088, 1024), BF), pltpu.VMEM((1024, 2304), BF),
            pltpu.VMEM((1024, 320), BF), pltpu.VMEM((4, 256, 1024), F32),
            pltpu.SemaphoreType.DMA((11,)), pltpu.SemaphoreType.DMA((6,)),
        ],
        compiler_params=params(60),
        cost_estimate=pl.CostEstimate(flops=20_000_000_000, bytes_accessed=16 * MIB, transcendentals=0),
        name="near",
    )(near_offset, leaf_partner, leaf_count, unknowns, near_blocks, leaf_blocks, bt, inner_prev, inner_next)

    return pl.pallas_call(
        last_kernel,
        in_specs=[HBM] * 8,
        out_specs=HBM,
        out_shape=acc_shape,
        scratch_shapes=[
            pltpu.VMEM((1088, 1024), BF), pltpu.VMEM((1024, 1280), BF), pltpu.VMEM((1024, 320), BF),
            pltpu.VMEM((4, 256, 1024), F32), pltpu.VMEM((LEVEL, 64, 256), BF), pltpu.VMEM((256, 64), BF),
            pltpu.VMEM((64, 64), BF), pltpu.VMEM((4, 64, 256), BF), pltpu.VMEM((4, 256, 1024), F32),
            pltpu.SemaphoreType.DMA((11,)), pltpu.SemaphoreType.DMA((4,)),
        ],
        compiler_params=params(60),
        name="product",
    )(cross, blocks, left, acc, fields, lt, pt, bt)


def solution(mesh):
    return jax.shard_map(
        body,
        mesh=mesh,
        in_specs=(
            P(("leaf", "level"), None, None),
            P(("leaf", "level"), None, None),
            P(("leaf", "level"), None, None),
            P(("leaf", "level"), None, None),
            P(("leaf", "level"), None, None, None),
            P(("leaf", "level"), None),
            P(("leaf", "level"), None, None, None),
            P(("leaf", "level"), None),
            P(("leaf", "level")),
            P("leaf", "level", None, None),
            P("leaf", None),
            P("leaf"),
        ),
        out_specs=P(("leaf", "level"), None, None),
        check_vma=False,
    )
```

time: 202 us -> 106 us (0.52)
  waiting for transfers between devices: 77.2 us -> 17 us
  local copies, waits for them, and re-layouts: 46.5 us -> 2.51 us
  Pallas kernels: 0 us -> 34.8 us
  matrix products: 26.1 us -> 0 us
  between operations: 14.2 us -> 0.98 us
  blocking collectives: 20.6 us -> 33.5 us
  starting transfers between devices: 5.91 us -> 16.5 us
  other arithmetic: 10.2 us -> 0 us
    all_gather x1 -> x0, waiting for transfers between devices: 74.3 us -> none  [body(): all_roots = lax.all_gather(root_moment[None], 'leaf', axis=0, tiled=True)]
    gather x4 -> x0, local copies, waits for them, and re-layouts: 40.9 us -> none  [the longest x2 31.9 us: body(): near_rows = jnp.take(window[:, :leaf_size], centre + near_offset, axis=0)]
    pallas_call x0 -> x7, Pallas kernels: none -> 34.8 us  [the longest x1 13 us: body(): pl.pallas_call(near_kernel, in_specs=[SMEM] * 3 + [HBM] * 6, out_specs=[H...]
    all_to_all x0 -> x2, blocking collectives: none -> 33.5 us  [the longest x1 20.5 us: body(): lax.all_to_all(root, 'leaf', 0, 0, axis_index_groups=groups, tiled=True)]
    dot_general x7 -> x0, matrix products: 26.1 us -> none  [the longest x1 11.9 us: body(): jnp.einsum('gsab,gsbn->gan', near_blocks, near_rows, preferred_element_ty...]
    psum x1 -> x0, blocking collectives: 20.6 us -> none  [body(): root_moment = lax.psum(root_terms, 'level').astype(jnp.bfloat16)]
    all_to_all x0 -> x1, waiting for transfers between devices: none -> 8.84 us  [body(): fields = lax.all_to_all(field, 'level', 0, 0, tiled=True)]
    ppermute x2 -> x10, waiting for transfers between devices: 0.01 us -> 8.17 us  [the longest x3 7.42 us: body(): lax.ppermute(column, 'leaf', along_x(step))]
  transfers between devices with their start and end apart: 4 -> 11, of which waited for: 2 -> 5; matrix products, arithmetic and copies ran while one was open for 27% -> 0% of each run, Pallas kernels for 0% -> 20%
where the time goes in v1:
time: 106 us; the launch traced here: 105 us
  Pallas kernels  34.8 us (33%)
  blocking collectives  33.5 us (32%)
  waiting for transfers between devices  17 us (16%)
  starting transfers between devices  16.5 us (16%)
  local copies, waits for them, and re-layouts  2.51 us (2%)
    all_to_all x1, blocking collectives, body(): lax.all_to_all(root, 'leaf', 0, 0, axis_index_groups=groups, tiled=True)  20.5 us
    pallas_call x1, Pallas kernels, body(): pl.pallas_call(near_kernel, in_specs=[SMEM] * 3 + [HBM] * 6, out_specs=[H...  13 us
    all_to_all x1, blocking collectives, body(): heap = lax.all_to_all(pieces, 'level', 0, 0, tiled=True)  13 us
    pallas_call x1, Pallas kernels, body(): pl.pallas_call(last_kernel, in_specs=[HBM] * 8, out_specs=HBM, out_shape=...  10 us
    all_to_all x1, waiting for transfers between devices, body(): fields = lax.all_to_all(field, 'level', 0, 0, tiled=True)  8.84 us
    ppermute x3, waiting for transfers between devices, body(): lax.ppermute(column, 'leaf', along_x(step))  7.42 us
    ppermute x3, starting transfers between devices, body(): lax.ppermute(column, 'leaf', along_x(step))  4.75 us
    ppermute x1, starting transfers between devices, body(): inner_prev = lax.ppermute(message, both, inner(ahead))  3.89 us
  transfers between devices with their start and end apart: 11, of which 5 were waited for; matrix products, arithmetic and copies ran while one was open for 0% of the time, Pallas kernels for 20%

profile of v1, /device:TPU:2, one launch (start us, length us, event | category | flops | bytes accessed | tf_op | source)
XLA Modules:
  0.0 105.3 jit_solution(14687189482828231508)
XLA Ops:
  0.0 3.4 %moments.1 = (bf16[4,208,256]{2,1,0:T(8,128)(2,1)}, bf16[1088,1024]{1,0:T(8,128)(2,1)}) custom-call(bf16[4,256,1024]{2,1,0:T(8,128)(2,1)} %u_hbm.1, bf16[4,64,256]{2,1,0:T(8,128)(2,1)} %bitcast.4, bf16[256,64]{1,0:T(8,128)(2,1)} %bitcast.8, bf16[64,64]{1,0:T(8,128)(2,1)} %bitcast.11, bf16[8,64,64]{2,1,0:T(8,128)(2,1)} %bitcast.10), custom_call_target="tpu_custom_call" | custom-call | tf_op jit(solution)/shard_map/moments/pallas_call | solution.py:324
  3.4 13.0 %all_to_all.15.refs_1_.msg_ref = bf16[4,208,256]{2,1,0:T(8,128)(2,1)} all-to-all(bf16[4,208,256]{2,1,0:T(8,128)(2,1)} %get-tuple-element.10), channel_id=1, replica_groups=mesh['leaf'=64,'level'=4] {'level'}, dimensions={0} | all-to-all | bytes 851968 | tf_op jit(solution)/shard_map/all_to_all | solution.py:338
  16.4 3.9 %collective-permute-start.2 = (bf16[1088,1024]{1,0:T(8,128)(2,1)}, bf16[1088,1024]{1,0:T(8,128)(2,1)}, u32[]{:S(2)}, u32[]{:S(2)}) collective-permute-start(bf16[1088,1024]{1,0:T(8,128)(2,1)} %send_inner.1.after_ref), channel_id=1, source_target_pairs={{0,1},{1,2},{2,3},{3,4},{4,5},{5,6},{6,7},{8,9},{9,10},{10,11},{11... | collective-permute-start | bytes 6684680 | tf_op jit(solution)/shard_map/ppermute | solution.py:342
  20.3 1.3 %collective-permute-start.3 = (bf16[1088,1024]{1,0:T(8,128)(2,1)}, bf16[1088,1024]{1,0:T(8,128)(2,1)}, u32[]{:S(2)}, u32[]{:S(2)}) collective-permute-start(bf16[1088,1024]{1,0:T(8,128)(2,1)} %send_inner.1.after_ref), channel_id=1, source_target_pairs={{1,0},{2,1},{3,2},{4,3},{5,4},{6,5},{7,6},{9,8},{10,9},{11,10},{12... | collective-permute-start | bytes 6684680 | tf_op jit(solution)/shard_map/ppermute | solution.py:343
  21.6 1.9 %roots.1 = bf16[8,64,256]{2,1,0:T(8,128)(2,1)} custom-call(bf16[4,208,256]{2,1,0:T(8,128)(2,1)} %all_to_all.15.refs_1_.msg_ref, bf16[1088,1024]{1,0:T(8,128)(2,1)} %send_inner.1.after_ref), custom_call_target="tpu_custom_call" | custom-call | tf_op jit(solution)/shard_map/roots/pallas_call | solution.py:345
  23.5 20.5 %all_to_all.16.own0 = bf16[8,64,256]{2,1,0:T(8,128)(2,1)S(1)} all-to-all(bf16[8,64,256]{2,1,0:T(8,128)(2,1)} %roots.1), channel_id=1, replica_groups={{0,8,16,24,32,40,48,56},{4,12,20,28,36,44,52,60},{64,72,80,88,96,104,11..., dimensions={0} | all-to-all | bytes 524288 | tf_op jit(solution)/shard_map/all_to_all | solution.py:362
  44.1 1.5 %collective-permute-start = (bf16[8,64,256]{2,1,0:T(8,128)(2,1)S(1)}, bf16[8,64,256]{2,1,0:T(8,128)(2,1)S(1)}, u32[]{:S(2)}, u32[]{:S(2)}) collective-permute-start(bf16[8,64,256]{2,1,0:T(8,128)(2,1)S(1)} %all_to_all.16.own0), channel_id=1, source_target_pairs={{0,64},{4,68},{8,72},{12,76},{16,80},{20,84},{24,88},{28,92},{32,9... | collective-permute-start | bytes 786440 | tf_op jit(solution)/shard_map/ppermute | solution.py:363
  45.6 1.1 %collective-permute-start.4 = (bf16[8,64,256]{2,1,0:T(8,128)(2,1)S(1)}, bf16[8,64,256]{2,1,0:T(8,128)(2,1)S(1)}, u32[]{:S(2)}, u32[]{:S(2)}) collective-permute-start(bf16[8,64,256]{2,1,0:T(8,128)(2,1)S(1)} %all_to_all.16.own0), channel_id=1, source_target_pairs={{0,128},{4,132},{8,136},{12,140},{16,144},{20,148},{24,152},{28,15... | collective-permute-start | bytes 786440 | tf_op jit(solution)/shard_map/ppermute | solution.py:363
  46.7 2.1 %collective-permute-start.5 = (bf16[8,64,256]{2,1,0:T(8,128)(2,1)S(1)}, bf16[8,64,256]{2,1,0:T(8,128)(2,1)S(1)}, u32[]{:S(2)}, u32[]{:S(2)}) collective-permute-start(bf16[8,64,256]{2,1,0:T(8,128)(2,1)S(1)} %all_to_all.16.own0), channel_id=1, source_target_pairs={{0,192},{4,196},{8,200},{12,204},{16,208},{20,212},{24,216},{28,22... | collective-permute-start | bytes 786440 | tf_op jit(solution)/shard_map/ppermute | solution.py:363
  48.8 4.5 %collective-permute-done.after_ref.own1 = bf16[8,64,256]{2,1,0:T(8,128)(2,1)S(1)} collective-permute-done((bf16[8,64,256]{2,1,0:T(8,128)(2,1)S(1)}, bf16[8,64,256]{2,1,0:T(8,128)(2,1)S(1)}, u32[]{:S(2)}, u32[]{:S(2)}) %collective-permute-start) | collective-permute-done | bytes 262176 | tf_op jit(solution)/shard_map/ppermute | solution.py:363
  53.3 0.0 collective-permute-start.6
  53.3 2.9 %collective-permute-done.4.own2 = bf16[8,64,256]{2,1,0:T(8,128)(2,1)S(1)} collective-permute-done((bf16[8,64,256]{2,1,0:T(8,128)(2,1)S(1)}, bf16[8,64,256]{2,1,0:T(8,128)(2,1)S(1)}, u32[]{:S(2)}, u32[]{:S(2)}) %collective-permute-start.4) | collective-permute-done | bytes 262176 | tf_op jit(solution)/shard_map/ppermute | solution.py:363
  56.3 0.0 collective-permute-start.7
  56.3 2.8 %send_crossing.1 = bf16[1088,1024]{1,0:T(8,128)(2,1)} custom-call(bf16[4,256,1024]{2,1,0:T(8,128)(2,1)} %u_hbm.1, bf16[4,64,256]{2,1,0:T(8,128)(2,1)} %bitcast.5, bf16[8,64,256]{2,1,0:T(8,128)(2,1)} %copy-done.1), custom_call_target="tpu_custom_call" | custom-call | tf_op jit(solution)/shard_map/send_crossing/pallas_call | solution.py:366
  59.1 0.0 collective-permute-done.5.own3
  59.1 2.5 %collective-permute-start.1 = (bf16[1088,1024]{1,0:T(8,128)(2,1)}, bf16[1088,1024]{1,0:T(8,128)(2,1)S(1)}, u32[]{:S(2)}, u32[]{:S(2)}) collective-permute-start(bf16[1088,1024]{1,0:T(8,128)(2,1)} %send_crossing.1), channel_id=1, source_target_pairs={{7,8},{15,16},{23,24},{31,32},{39,40},{47,48},{55,56},{63,64},{71,... | collective-permute-start | bytes 6684680 | tf_op jit(solution)/shard_map/ppermute | solution.py:375
  61.6 0.0 collective-permute-done.6.other0
  61.6 0.1 collective-permute-start.8
  61.7 0.0 collective-permute-done.7.other1
  61.7 0.5 collective-permute-start.9
  62.8 0.4 collective-permute-done.8.other2
  63.2 0.4 collective-permute-done.9.other3
  63.6 0.3 copy-done.8
  63.9 0.7 copy-done.9
  64.6 3.6 %top.1 = bf16[4,64,256]{2,1,0:T(8,128)(2,1)} custom-call(s32[1,32]{1,0:T(1,128)} %source_ref.1, s32[1]{0:T(128)S(6)} %copy.15.count_ref, bf16[8,64,256]{2,1,0:T(8,128)(2,1)} %copy-done.2, bf16[8,64,256]{2,1,0:T(8,128)(2,1)} %copy-done.1, bf16[8,64,256]{2,1,0:T(8,128)(2,1)} %copy-done.4, bf16[8,64,256]{2,1,0:T(8,128)(2,1)} %copy-done.5, ...), custom_call_target="tpu_custom_call" | custom-call | tf_op jit(solution)/shard_map/top/pallas_call | solution.py:377
  68.3 3.5 %all-to-all-start.2 = ((bf16[4,64,256]{2,1,0:T(8,128)(2,1)}), bf16[4,64,256]{2,1,0:T(8,128)(2,1)S(1)}, u32[]{:S(2)}, u32[]{:S(2)}) async-start(bf16[4,64,256]{2,1,0:T(8,128)(2,1)} %top.1), calls=%async_computation.2 | async-start | bytes 262144 | tf_op jit(solution)/shard_map/all_to_all | solution.py:389
  71.8 0.0 collective-permute-done.2.p_hbm
  71.8 13.0 %near.1 = (f32[4,256,1024]{2,1,0:T(8,128)}, bf16[1024,1280]{1,0:T(8,128)(2,1)}, bf16[1024,320]{1,0:T(8,128)(2,1)}) custom-call(s32[4,8]{1,0:T(4,128)} %offset_ref.1, s32[4,6]{1,0:T(4,128)} %partner_ref.1, s32[4]{0:T(128)} %count_ref.2, bf16[4,256,1024]{2,1,0:T(8,128)(2,1)} %u_hbm.1, bf16[4,8,256,256]{3,2,1,0:T(8,128)(2,1)} %nb_hbm.1, ...), custom_call_target="tpu_custom_call" | custom-call | flops 20000000000 | bytes 16777216 | tf_op jit(solution)/shard_map/near/pallas_call | solution.py:391
  84.8 8.8 %all-to-all-done.2.field_hbm = bf16[4,64,256]{2,1,0:T(8,128)(2,1)S(1)} async-done(((bf16[4,64,256]{2,1,0:T(8,128)(2,1)}), bf16[4,64,256]{2,1,0:T(8,128)(2,1)S(1)}, u32[]{:S(2)}, u32[]{:S(2)}) %all-to-all-start.2) | async-done | bytes 131104 | tf_op jit(solution)/shard_map/all_to_all | solution.py:389
  93.7 0.6 copy-done.3
  94.3 0.8 copy-done
  95.1 10.0 %product.1 = f32[4,256,1024]{2,1,0:T(8,128)} custom-call(bf16[1088,1024]{1,0:T(8,128)(2,1)} %copy-done, bf16[1024,1280]{1,0:T(8,128)(2,1)} %get-tuple-element.12.blocks_hbm, bf16[1024,320]{1,0:T(8,128)(2,1)} %get-tuple-element.13.left_hbm, f32[4,256,1024]{2,1,0:T(8,128)} %get-tuple-element.14.acc_hbm, bf16[4,64,256]{2,1,0:T(8,128)(2,1)} %copy-done.3, ...), custom_call_target="tpu_custom_call" | custom-call | tf_op jit(solution)/shard_map/product/pallas_call | solution.py:410
  (19 shorter events, 0.0 us)
Async XLA Ops:
  16.4 55.3 %collective-permute-start.2 = (bf16[1088,1024]{1,0:T(8,128)(2,1)}, bf16[1088,1024]{1,0:T(8,128)(2,1)}, u32[]{:S(2)}, u32[]{:S(2)}) collective-permute-start(bf16[1088,1024]{1,0:T(8,128)(2,1)} %send_inner.1.after_ref), channel_id=1, source_target_pairs={{0,1},{1,2},{2,3},{3,4},{4,5},{5,6},{6,7},{8,9},{9,10},{10,11},{11... | collective-permute-start | bytes 6684680 | tf_op jit(solution)/shard_map/ppermute | solution.py:342
  20.3 51.5 %collective-permute-start.3 = (bf16[1088,1024]{1,0:T(8,128)(2,1)}, bf16[1088,1024]{1,0:T(8,128)(2,1)}, u32[]{:S(2)}, u32[]{:S(2)}) collective-permute-start(bf16[1088,1024]{1,0:T(8,128)(2,1)} %send_inner.1.after_ref), channel_id=1, source_target_pairs={{1,0},{2,1},{3,2},{4,3},{5,4},{6,5},{7,6},{9,8},{10,9},{11,10},{12... | collective-permute-start | bytes 6684680 | tf_op jit(solution)/shard_map/ppermute | solution.py:343
  44.1 19.5 %copy-start.2 = (bf16[8,64,256]{2,1,0:T(8,128)(2,1)}, bf16[8,64,256]{2,1,0:T(8,128)(2,1)S(1)}, u32[]{:S(2)}) copy-start(bf16[8,64,256]{2,1,0:T(8,128)(2,1)S(1)} %all_to_all.16.own0) | copy-start | bytes 786436
  44.1 9.2 %collective-permute-start = (bf16[8,64,256]{2,1,0:T(8,128)(2,1)S(1)}, bf16[8,64,256]{2,1,0:T(8,128)(2,1)S(1)}, u32[]{:S(2)}, u32[]{:S(2)}) collective-permute-start(bf16[8,64,256]{2,1,0:T(8,128)(2,1)S(1)} %all_to_all.16.own0), channel_id=1, source_target_pairs={{0,64},{4,68},{8,72},{12,76},{16,80},{20,84},{24,88},{28,92},{32,9... | collective-permute-start | bytes 786440 | tf_op jit(solution)/shard_map/ppermute | solution.py:363
  45.6 10.7 %collective-permute-start.4 = (bf16[8,64,256]{2,1,0:T(8,128)(2,1)S(1)}, bf16[8,64,256]{2,1,0:T(8,128)(2,1)S(1)}, u32[]{:S(2)}, u32[]{:S(2)}) collective-permute-start(bf16[8,64,256]{2,1,0:T(8,128)(2,1)S(1)} %all_to_all.16.own0), channel_id=1, source_target_pairs={{0,128},{4,132},{8,136},{12,140},{16,144},{20,148},{24,152},{28,15... | collective-permute-start | bytes 786440 | tf_op jit(solution)/shard_map/ppermute | solution.py:363
  46.7 12.4 %collective-permute-start.5 = (bf16[8,64,256]{2,1,0:T(8,128)(2,1)S(1)}, bf16[8,64,256]{2,1,0:T(8,128)(2,1)S(1)}, u32[]{:S(2)}, u32[]{:S(2)}) collective-permute-start(bf16[8,64,256]{2,1,0:T(8,128)(2,1)S(1)} %all_to_all.16.own0), channel_id=1, source_target_pairs={{0,192},{4,196},{8,200},{12,204},{16,208},{20,212},{24,216},{28,22... | collective-permute-start | bytes 786440 | tf_op jit(solution)/shard_map/ppermute | solution.py:363
  53.3 2.9 %copy-start.1 = (bf16[8,64,256]{2,1,0:T(8,128)(2,1)}, bf16[8,64,256]{2,1,0:T(8,128)(2,1)S(1)}, u32[]{:S(2)}) copy-start(bf16[8,64,256]{2,1,0:T(8,128)(2,1)S(1)} %collective-permute-done.after_ref.own1) | copy-start | bytes 786436
  53.3 8.2 %collective-permute-start.6 = (bf16[8,64,256]{2,1,0:T(8,128)(2,1)S(1)}, bf16[8,64,256]{2,1,0:T(8,128)(2,1)S(1)}, u32[]{:S(2)}, u32[]{:S(2)}) collective-permute-start(bf16[8,64,256]{2,1,0:T(8,128)(2,1)S(1)} %all_to_all.16.own0), channel_id=1, source_target_pairs={{0,4},{4,0},{8,12},{12,8},{16,20},{20,16},{24,28},{28,24},{32,36},... | collective-permute-start | bytes 786440 | tf_op jit(solution)/shard_map/ppermute | solution.py:364
  56.3 5.3 %copy-start.4 = (bf16[8,64,256]{2,1,0:T(8,128)(2,1)}, bf16[8,64,256]{2,1,0:T(8,128)(2,1)S(1)}, u32[]{:S(2)}) copy-start(bf16[8,64,256]{2,1,0:T(8,128)(2,1)S(1)} %collective-permute-done.4.own2) | copy-start | bytes 786436
  56.3 5.4 %collective-permute-start.7 = (bf16[8,64,256]{2,1,0:T(8,128)(2,1)S(1)}, bf16[8,64,256]{2,1,0:T(8,128)(2,1)S(1)}, u32[]{:S(2)}, u32[]{:S(2)}) collective-permute-start(bf16[8,64,256]{2,1,0:T(8,128)(2,1)S(1)} %collective-permute-done.after_ref.own1), channel_id=1, source_target_pairs={{0,4},{4,0},{8,12},{12,8},{16,20},{20,16},{24,28},{28,24},{32,36},... | collective-permute-start | bytes 786440 | tf_op jit(solution)/shard_map/ppermute | solution.py:364
  59.1 4.5 %copy-start.5 = (bf16[8,64,256]{2,1,0:T(8,128)(2,1)}, bf16[8,64,256]{2,1,0:T(8,128)(2,1)S(1)}, u32[]{:S(2)}) copy-start(bf16[8,64,256]{2,1,0:T(8,128)(2,1)S(1)} %collective-permute-done.5.own3) | copy-start | bytes 786436
  59.1 34.6 %collective-permute-start.1 = (bf16[1088,1024]{1,0:T(8,128)(2,1)}, bf16[1088,1024]{1,0:T(8,128)(2,1)S(1)}, u32[]{:S(2)}, u32[]{:S(2)}) collective-permute-start(bf16[1088,1024]{1,0:T(8,128)(2,1)} %send_crossing.1), channel_id=1, source_target_pairs={{7,8},{15,16},{23,24},{31,32},{39,40},{47,48},{55,56},{63,64},{71,... | collective-permute-start | bytes 6684680 | tf_op jit(solution)/shard_map/ppermute | solution.py:375
  61.6 2.0 %copy-start.6 = (bf16[8,64,256]{2,1,0:T(8,128)(2,1)}, bf16[8,64,256]{2,1,0:T(8,128)(2,1)S(1)}, u32[]{:S(2)}) copy-start(bf16[8,64,256]{2,1,0:T(8,128)(2,1)S(1)} %collective-permute-done.6.other0) | copy-start | bytes 786436
  61.6 1.6 %collective-permute-start.8 = (bf16[8,64,256]{2,1,0:T(8,128)(2,1)S(1)}, bf16[8,64,256]{2,1,0:T(8,128)(2,1)S(1)}, u32[]{:S(2)}, u32[]{:S(2)}) collective-permute-start(bf16[8,64,256]{2,1,0:T(8,128)(2,1)S(1)} %collective-permute-done.4.own2), channel_id=1, source_target_pairs={{0,4},{4,0},{8,12},{12,8},{16,20},{20,16},{24,28},{28,24},{32,36},... | collective-permute-start | bytes 786440 | tf_op jit(solution)/shard_map/ppermute | solution.py:364
  61.7 1.9 %copy-start.7 = (bf16[8,64,256]{2,1,0:T(8,128)(2,1)}, bf16[8,64,256]{2,1,0:T(8,128)(2,1)S(1)}, u32[]{:S(2)}) copy-start(bf16[8,64,256]{2,1,0:T(8,128)(2,1)S(1)} %collective-permute-done.7.other1) | copy-start | bytes 786436
  61.7 1.9 %collective-permute-start.9 = (bf16[8,64,256]{2,1,0:T(8,128)(2,1)S(1)}, bf16[8,64,256]{2,1,0:T(8,128)(2,1)S(1)}, u32[]{:S(2)}, u32[]{:S(2)}) collective-permute-start(bf16[8,64,256]{2,1,0:T(8,128)(2,1)S(1)} %collective-permute-done.5.own3), channel_id=1, source_target_pairs={{0,4},{4,0},{8,12},{12,8},{16,20},{20,16},{24,28},{28,24},{32,36},... | collective-permute-start | bytes 786440 | tf_op jit(solution)/shard_map/ppermute | solution.py:364
  63.2 0.7 copy-start.8
  63.9 0.7 copy-start.9
  68.3 25.4 %all-to-all-start.2 = ((bf16[4,64,256]{2,1,0:T(8,128)(2,1)}), bf16[4,64,256]{2,1,0:T(8,128)(2,1)S(1)}, u32[]{:S(2)}, u32[]{:S(2)}) async-start(bf16[4,64,256]{2,1,0:T(8,128)(2,1)} %top.1), calls=%async_computation.2 | async-start | bytes 262144 | tf_op jit(solution)/shard_map/all_to_all | solution.py:389
  93.7 0.7 copy-start.3
  93.7 1.5 %copy-start = (bf16[1088,1024]{1,0:T(8,128)(2,1)}, bf16[1088,1024]{1,0:T(8,128)(2,1)S(1)}, u32[]{:S(2)}) copy-start(bf16[1088,1024]{1,0:T(8,128)(2,1)S(1)} %collective-permute-done.1.cross_hbm) | copy-start | bytes 6684676
